TPU v7x, 128 devices: a whole 4x4x4 slice. The times are simulated.
128 devices in a mesh: dp: 8 (over x_hi, z), tensor: 16 (over x_lo, y, core).
Axes of the slice: x: 4 (x_hi: 2, x_lo: 2; x = x_hi * 2 + x_lo), y: 4, z: 4, core: 2. Of those that a mesh axis runs over, the one named last changes fastest.
Arguments:
- history: bfloat16 [17, 16384, 2048], P(None, ('dp', 'tensor')), may hold values from -6 to 6
- cotangent: bfloat16 [16384, 2048], P(('dp', 'tensor')), may hold values from -6 to 6
- lengths: int32 [8, 4], replicated, may hold values from 0 to 2048, as said below
- mix_gain: float32 [2048], replicated, may hold values from 0.5 to 1.5
- mix_first: float32 [2048, 68], replicated, may hold values from -0.125 to 0.125
- mix_second: float32 [68, 68], replicated, may hold values from -0.3 to 0.3
- mix_bias: float32 [68], replicated, may hold values from -1.8 to 1.8
- gain_query: float32 [2048], replicated, may hold values from 0.5 to 1.5
- gain_key: float32 [2048], replicated, may hold values from 0.5 to 1.5
- gain_value: float32 [2048], replicated, may hold values from 0.5 to 1.5
- gain_mlp: float32 [2048], replicated, may hold values from 0.5 to 1.5
- w_query: bfloat16 [2048, 2048], P(None, 'tensor'), may hold values from -0.125 to 0.125
- w_key: bfloat16 [2048, 2048], P(None, 'tensor'), may hold values from -0.125 to 0.125
- w_value: bfloat16 [2048, 2048], P(None, 'tensor'), may hold values from -0.125 to 0.125
- w_output: bfloat16 [2048, 2048], P('tensor'), may hold values from -1 to 1
- w_expand: bfloat16 [2048, 8192], P(None, 'tensor'), may hold values from -0.125 to 0.125
- w_reduce: bfloat16 [8192, 2048], P('tensor'), may hold values from -0.0625 to 0.0625
Outputs:
- output: bfloat16 [16384, 2048], P(('dp', 'tensor'))
- grad_history: bfloat16 [17, 16384, 2048], P(None, ('dp', 'tensor'))
- grad_mix_gain: float32 [2048], replicated
- grad_mix_first: float32 [2048, 68], replicated
- grad_mix_second: float32 [68, 68], replicated
- grad_mix_bias: float32 [68], replicated
- grad_gain_query: float32 [2048], replicated
- grad_gain_key: float32 [2048], replicated
- grad_gain_value: float32 [2048], replicated
- grad_gain_mlp: float32 [2048], replicated
- grad_w_query: float32 [2048, 2048], P('dp', 'tensor')
- grad_w_key: float32 [2048, 2048], P('dp', 'tensor')
- grad_w_value: float32 [2048, 2048], P('dp', 'tensor')
- grad_w_output: float32 [2048, 2048], P('tensor', 'dp')
- grad_w_expand: float32 [2048, 8192], P('dp', 'tensor')
- grad_w_reduce: float32 [8192, 2048], P('tensor', 'dp')
Inputs may be any that keep to these rules, and one draw needn't show every extreme that they name: Row g holds, in order, the lengths of the sequences packed into the 2048 tokens of data index g (0 marks an empty slot); each row sums to 2048, its longest entry is 1024 or more, and in some row one sequence fills all 2048 tokens.
All inputs are finite; a program needn't handle non-finite values.
Results may differ from a plain program's by a relative error of at most 0.019.
Values may be sent and summed in bfloat16 or wider, within the bound.
A program may use at most 320 MiB of HBM per device.

v0:
```python
import functools

import jax
import jax.numpy as jnp
from jax import lax
from jax.experimental import pallas as pl
from jax.experimental.pallas import tpu as pltpu
from jax.sharding import PartitionSpec as P

HEAD_DIM = 128
HISTORY = 17
STREAMS = 4
MIX = HISTORY * STREAMS
D = 2048
ROWS = 128
FF_SHARD = 512
NORM_EPS = 1e-06
MASKED = -1e30
EXPONENT = HEAD_DIM ** (-0.5) * 1.4426950408889634
MESH = pl.DeviceIdType.MESH
BF = jnp.bfloat16
F32 = jnp.float32
VMEM = pltpu.VMEM
ANY = pl.ANY
MIB = 2**20

Y1, Y2, Y3 = 2, 4, 6
SIB, XN, DIAG = 1, 8, 9
A_MASKS = (0, SIB, XN, DIAG)
LO, HI = pl.ds(0, 64), pl.ds(64, 64)


def flip(value, mask):
    for bit in (1, 2, 4, 8):
        if mask & bit:
            value = value + bit - 2 * bit * lax.rem(lax.div(value, bit), 2)
    return value


def dev(t_mask, dp_mask=0):
    return (flip(lax.axis_index("dp"), dp_mask), flip(lax.axis_index("tensor"), t_mask))


def enter(partners):
    barrier = pltpu.get_barrier_semaphore()
    for partner in partners:
        pl.semaphore_signal(barrier, inc=1, device_id=dev(*partner), device_id_type=MESH)
    pl.semaphore_wait(barrier, len(partners))


def rcopy(src, dst, send, recv, target):
    return pltpu.make_async_remote_copy(
        src_ref=src, dst_ref=dst, send_sem=send, recv_sem=recv, device_id=dev(*target), device_id_type=MESH
    )


def nt(a, b):
    return lax.dot_general(a, b, (((1,), (1,)), ((), ())), preferred_element_type=F32)


def tn(a, b):
    return lax.dot_general(a, b, (((0,), (0,)), ((), ())), preferred_element_type=F32)


def nn(a, b):
    return jnp.dot(a, b, preferred_element_type=F32)


class Gather:
    def __init__(self, own, rows, send, recv, slots=(0, 1, 2, 3)):
        def c(i, src, dst, target):
            return rcopy(src, dst, send.at[i], recv.at[i], (target,))

        _, one, two, three = slots
        self.copies = [
            c(0, own.at[LO], rows.at[one, LO], Y1),
            c(1, own.at[HI], rows.at[three, HI], Y3),
            c(2, own.at[HI], rows.at[one, HI], Y1),
            c(3, own.at[LO], rows.at[three, LO], Y3),
            c(4, rows.at[one, LO], rows.at[two, LO], Y3),
            c(5, rows.at[three, HI], rows.at[two, HI], Y1),
        ]

    def start(self):
        for i in range(4):
            self.copies[i].start()

    def forward(self):
        self.copies[0].wait_recv()
        self.copies[4].start()
        self.copies[1].wait_recv()
        self.copies[5].start()

    def arrived(self, slot):
        for i in {1: (2,), 3: (3,), 2: (4, 5)}[slot]:
            self.copies[i].wait_recv()

    def finish(self):
        for c in self.copies:
            c.wait_send()


def halves(value):
    high = value.astype(BF)
    return high, (value - high.astype(F32)).astype(BF)


def exact(a, b, dims):
    (ah, am), (bh, bm) = halves(a), halves(b)

    def dot(x, y):
        return lax.dot_general(x, y, (dims, ((), ())), preferred_element_type=F32)

    return dot(ah, bh) + (dot(ah, bm) + dot(am, bh))


def gelu_parts(x):
    cdf = 0.5 * (1.0 + lax.erf(x * (0.5**0.5)))
    return x * cdf, cdf + x * jnp.exp(-0.5 * x * x) * 0.3989422804014327


STEP = 16
WIDE = 256


def mix_tokens(last, mix_gain, mix_first, mix_second, mix_bias, pre_out, mix_out):
    inverse = lax.rsqrt(jnp.mean(last * last, axis=-1, keepdims=True) + NORM_EPS)
    pre = exact(last * inverse * mix_gain[...], mix_first[...], ((1,), (1,)))
    pre_out[...] = pre
    hidden = gelu_parts(pre)[0]
    mix_out[...] = exact(hidden, mix_second[...], ((1,), (0,))) + mix_bias[...]


def make_streams(at, hist, mix, gains, held, x_out, n_out, inv_out, resid_out):
    here = mix[at]
    lane = lax.broadcasted_iota(jnp.int32, (STEP, 128), 1)
    own = lax.rem(lane, STEP) == lax.broadcasted_iota(jnp.int32, (STEP, 128), 0)
    entry = lax.div(lane, STEP)
    high, low = [], []
    for k in range(STREAMS):
        pieces = []
        for part in range(2):
            piece = jnp.zeros((STEP, 128), F32)
            for j in range(8):
                i = k * HISTORY + part * 8 + j
                piece = jnp.where(entry == j, here[:, i : i + 1], piece)
            pieces.append(jnp.where(own, piece, 0.0))
        h, m = halves(jnp.concatenate(pieces, axis=1))
        high.append(h)
        low.append(m)
    left = jnp.concatenate(high + low, axis=0)
    squares = [jnp.zeros((STEP, 1), F32) for _ in range(3)]
    for c in range(D // 512):
        cols = slice(c * 512, (c + 1) * 512)
        product = nn(left, hist[0 : HISTORY - 1, at, cols].reshape(256, 512))
        newest = hist[HISTORY - 1, at, cols].astype(F32)
        for k in range(STREAMS):
            i = k * HISTORY + HISTORY - 1
            value = product[k * STEP : (k + 1) * STEP] + product[(4 + k) * STEP : (5 + k) * STEP]
            value = value + here[:, i : i + 1] * newest
            if k == 3:
                resid_out[at, cols] = value
            else:
                held[k, :, cols] = value
                squares[k] = squares[k] + jnp.sum(value * value, axis=-1, keepdims=True)
    for k in range(3):
        inverse = lax.rsqrt(squares[k] * (1.0 / D) + NORM_EPS)
        inv_out[k, at] = jnp.broadcast_to(inverse, (STEP, 128))
        normal = held[k] * inverse
        n_out[k, at] = normal.astype(BF)
        x_out[k, at] = (normal * gains[k][...]).astype(BF)


def qkv_kernel(
    hist_in, cot, mix_gain, mix_first, mix_second, mix_bias, gain_q, gain_k, gain_v,
    w_query, w_key, w_value, w_output, w_expand,
    heads, rows_out, w_out, wo_all, we_two, cot_all, n_out, inv_out, resid_out, mix, pre,
    hist, held, x, rows, weights, proj, hist_sem, cot_send, cot_recv, g_send, g_recv, w_send, w_recv, f_send, f_recv, h_send, h_recv, local,
):
    tiles = ROWS // STEP
    latest = pltpu.make_async_copy(hist_in.at[HISTORY - 1], hist.at[HISTORY - 1], hist_sem.at[tiles])
    latest.start()
    older = pl.ds(0, HISTORY - 1)

    def tile_load(tile):
        at = pl.ds(pl.multiple_of(tile * STEP, STEP), STEP)
        return pltpu.make_async_copy(hist_in.at[older, at], hist.at[older, at], hist_sem.at[tile])

    for tile in range(tiles):
        tile_load(tile).start()
    enter([(Y1,), (Y3,), (SIB,), (XN,), (XN, 4), (DIAG,)])
    t = lax.axis_index("tensor")
    left = pl.ds(0, D // 2)
    cot_gather = Gather(cot.at[:, left], cot_all, cot_send, cot_recv, (0, 1, 3, 2))
    cot_gather.start()
    cot_keep = pltpu.make_async_copy(cot.at[:, left], cot_all.at[0], hist_sem.at[tiles + 1])
    cot_keep.start()
    sources = [w_query, w_key, w_value, w_output, w_expand]
    slots = [lambda r, i=i: weights.at[i, r] for i in range(3)]
    slots += [lambda r: wo_all.at[r], lambda r: we_two.at[r - 1]]
    to_sib, to_x, onward = [], [], []
    for i, src in enumerate(sources):
        half = src.shape[0] // 2
        lo, hi = pl.ds(0, half), pl.ds(half, half)
        to_x.append(
            (
                rcopy(src.at[lo], slots[i](2).at[lo], w_send.at[i, 0], w_recv.at[i, 0], (XN,)),
                rcopy(src.at[hi], slots[i](2).at[hi], w_send.at[i, 1], w_recv.at[i, 1], (XN, 4)),
            )
        )
        to_sib.append(rcopy(src, slots[i](1), w_send.at[i, 2], w_recv.at[i, 2], (SIB,)))
        if i < 4:
            onward.append(rcopy(slots[i](2), slots[i](3), f_send.at[i], f_recv.at[i], (SIB,)))
    keep = [pltpu.make_async_copy(sources[i], slots[i](0), local.at[i]) for i in range(4)]
    gathers = [Gather(x.at[a], rows.at[a], g_send.at[a], g_recv.at[a]) for a in range(3)]
    for a in range(3):
        to_x[a][0].start()
        to_x[a][1].start()
        to_sib[a].start()
        keep[a].start()
    latest.wait()
    mix_tokens(hist[HISTORY - 1].astype(F32), mix_gain, mix_first, mix_second, mix_bias, pre, mix)

    @pl.loop(0, tiles)
    def _(tile):
        tile_load(tile).wait()
        at = pl.ds(pl.multiple_of(tile * STEP, STEP), STEP)
        make_streams(at, hist, mix, (gain_q, gain_k, gain_v), held, x, n_out, inv_out, resid_out)

    cot_gather.forward()
    gathers[0].start()
    gathers[1].start()
    for i in (3, 4):
        to_x[i][0].start()
        to_x[i][1].start()
        to_sib[i].start()
    keep[3].start()
    for a in range(3):
        for c in to_x[a]:
            c.wait_recv()
        onward[a].start()
        gathers[a].forward()
        if a == 0:
            gathers[2].start()
    sends = []

    def project(a, s):
        block = x[a] if s == 0 else rows[a, s]
        for p in range(2):
            pair = jnp.concatenate([weights[a, 2 * p], weights[a, 2 * p + 1]], axis=1)
            y = nn(block, pair).astype(BF)
            proj[a, s, 2 * p] = y[:, :128]
            proj[a, s, 2 * p + 1] = y[:, 128:]
        place = flip(t, 2 * s)
        for r in range(4):
            src, dst = proj.at[a, s, r], heads.at[a, place]
            if r == 0:
                c = pltpu.make_async_copy(src, dst, h_send.at[a, s, 0])
            else:
                c = rcopy(src, dst, h_send.at[a, s, r], h_recv.at[a, s, r], (A_MASKS[r],))
            c.start()
            sends.append((r, c))

    for a in range(3):
        keep[a].wait()
        to_sib[a].wait_recv()
        onward[a].wait_recv()
        project(a, 0)
    store = []
    for a in range(3):
        c = pltpu.make_async_copy(weights.at[a], w_out.at[a], local.at[4 + a])
        c.start()
        store.append(c)
        c = pltpu.make_async_copy(x.at[a], rows_out.at[a, 0], local.at[7 + a])
        c.start()
        store.append(c)
    for a in range(3):
        for s in (1, 3):
            gathers[a].arrived(s)
            project(a, s)
    for c in to_x[3]:
        c.wait_recv()
    onward[3].start()
    for a in range(3):
        gathers[a].arrived(2)
        project(a, 2)
        c = pltpu.make_async_copy(rows.at[a, pl.ds(1, 3)], rows_out.at[a, pl.ds(1, 3)], local.at[10 + a])
        c.start()
        store.append(c)
    for s in (1, 3, 2):
        cot_gather.arrived(s)
    cot_keep.wait()
    for g in gathers + [cot_gather]:
        g.finish()
    for r, c in sends:
        if r == 0:
            c.wait()
        else:
            c.wait_send()
    for r, c in sends:
        if r:
            c.wait_recv()
    for i in range(5):
        for c in to_x[i]:
            c.wait_send()
            if i > 3:
                c.wait_recv()
        to_sib[i].wait_send()
        if i > 2:
            to_sib[i].wait_recv()
    for i in range(4):
        onward[i].wait_send()
    onward[3].wait_recv()
    keep[3].wait()
    for c in store:
        c.wait()


def qkv(history, cot, mix_gain, mix_first, mix_second, mix_bias, gains, *weights):
    dma = pltpu.SemaphoreType.DMA
    vm, hbm = pl.BlockSpec(memory_space=VMEM), pl.BlockSpec(memory_space=ANY)
    return pl.pallas_call(
        qkv_kernel,
        in_specs=[hbm] * 2 + [vm] * 7 + [hbm] * 5,
        out_specs=[hbm] * 6 + [vm] * 5,
        out_shape=[
            jax.ShapeDtypeStruct((3, 16, ROWS, HEAD_DIM), BF),
            jax.ShapeDtypeStruct((3, 4, ROWS, D), BF),
            jax.ShapeDtypeStruct((3, 4, D, HEAD_DIM), BF),
            jax.ShapeDtypeStruct((4, HEAD_DIM, D), BF),
            jax.ShapeDtypeStruct((2, D, FF_SHARD), BF),
            jax.ShapeDtypeStruct((4, ROWS, D // 2), BF),
            jax.ShapeDtypeStruct((3, ROWS, D), BF),
            jax.ShapeDtypeStruct((3, ROWS, 128), F32),
            jax.ShapeDtypeStruct((ROWS, D), F32),
            jax.ShapeDtypeStruct((ROWS, MIX), F32),
            jax.ShapeDtypeStruct((ROWS, MIX), F32),
        ],
        scratch_shapes=[
            VMEM((HISTORY, ROWS, D), BF),
            VMEM((3, STEP, D), F32),
            VMEM((3, ROWS, D), BF),
            VMEM((3, 4, ROWS, D), BF),
            VMEM((3, 4, D, HEAD_DIM), BF),
            VMEM((3, 4, 4, ROWS, HEAD_DIM), BF),
            dma((ROWS // STEP + 2,)), dma((6,)), dma((6,)),
            dma((3, 6)), dma((3, 6)), dma((5, 3)), dma((5, 3)), dma((4,)), dma((4,)), dma((3, 4, 4)), dma((3, 4, 4)), dma((13,)),
        ],
        compiler_params=pltpu.CompilerParams(collective_id=1, has_side_effects=True, vmem_limit_bytes=61 * MIB),
        cost_estimate=pl.CostEstimate(flops=6 * 512 * 2048 * 512, bytes_accessed=30 * MIB, transcendentals=0),
        name="qkv",
    )(
        history, cot, mix_gain[None], mix_first.T, mix_second, mix_bias[None], *[g[None] for g in gains], *weights
    )


def first_places(lengths, places):
    group = lax.axis_index("dp")
    first, end = jnp.zeros_like(places), jnp.int32(0)
    for i in range(lengths.shape[1]):
        end = end + lengths[group, i]
        first = jnp.where(places >= end, end, first)
    return first


def attend_kernel(q, k, v, lengths, ctx, hooks):
    tokens, step = q.shape[0], 256
    for i in range(tokens // step):
        if i in hooks:
            hooks[i]()
        length = (i + 1) * step
        at = slice(i * step, length)
        scores = nt(q[at], k[:length])
        key_place = lax.broadcasted_iota(jnp.int32, (step, length), 1)
        query_place = lax.broadcasted_iota(jnp.int32, (step, 1), 0) + i * step
        allowed = (key_place >= first_places(lengths, query_place)) & (key_place <= query_place)
        scores = jnp.where(allowed, scores, MASKED)
        top = jnp.max(scores, axis=-1, keepdims=True)
        e = jnp.exp2((scores - top) * EXPONENT)
        low = (e * (1.0 / jnp.sum(e, axis=-1, keepdims=True))).astype(BF)
        ctx[at] = nn(low, v[:length]).astype(BF)


def attend_back_kernel(q, k, v, gc, lengths, dq, dk, dv, dk_sum, dv_sum, hooks):
    tokens, step = q.shape[0], 256
    scale = HEAD_DIM ** (-0.5)
    k_turned = k[...].astype(F32).T.astype(BF)
    for i in range(tokens // step):
        if i in hooks:
            hooks[i]()
        length = (i + 1) * step
        at = slice(i * step, length)
        scores = nt(k[:length], q[at])
        key_place = lax.broadcasted_iota(jnp.int32, (length, step), 0)
        query_place = lax.broadcasted_iota(jnp.int32, (1, step), 1) + i * step
        allowed = (key_place >= first_places(lengths, query_place)) & (key_place <= query_place)
        scores = jnp.where(allowed, scores, MASKED)
        top = jnp.max(scores, axis=0, keepdims=True)
        e = jnp.exp2((scores - top) * EXPONENT)
        probs = e * (1.0 / jnp.sum(e, axis=0, keepdims=True))
        grad_probs = nt(v[:length], gc[at])
        delta = jnp.sum(grad_probs * probs, axis=0, keepdims=True)
        grad_scores = (probs * (grad_probs - delta)).astype(BF)
        low = probs.astype(BF)
        dq[at] = (nn(k_turned[:, :length], grad_scores) * scale).T.astype(BF)
        key_part = nn(grad_scores, q[at])
        value_part = nn(low, gc[at])
        if i:
            dk_sum[: i * step] += key_part[: i * step]
            dv_sum[: i * step] += value_part[: i * step]
        dk_sum[at] = key_part[i * step :]
        dv_sum[at] = value_part[i * step :]
    dk[...] = (dk_sum[...] * scale).astype(BF)
    dv[...] = dv_sum[...].astype(BF)


def mlp_kernel(
    heads, lengths, gain, wo_in, resid_in, cot, cot_all, w_expand, we_two, w_reduce,
    ctx_rows, middle_out, reduced_out, keep_out, grad_gain, grad_middle, grad_low,
    ctx, we, wr, mlp_rows, cot_rows, act, gexp, parts, stage, sc_out, sc_pass, sc_got,
    mlp_sib, cot_sib, act_sib, gexp_sib, act_turned,
    g_send, g_recv, s_send, s_recv, w_send, w_recv, c_send, c_recv, d_send, d_recv, local, keep_sem, cot_send, cot_recv,
    wo_all, resid, late_sem,
):
    late = [
        pltpu.make_async_copy(wo_in, wo_all, late_sem.at[0]),
        pltpu.make_async_copy(resid_in, resid, late_sem.at[1]),
    ]
    for c in late:
        c.start()
    enter([(Y1,), (Y3,), (SIB,), (XN,), (XN, 4), (DIAG,)])
    t = lax.axis_index("tensor")
    q, k, v = heads.at[0], heads.at[1], heads.at[2]
    slots = (0, 1, 3, 2)
    right = pl.ds(D // 2, D // 2)
    cot_gather = Gather(cot.at[:, right], cot_rows.at[:, :, right], cot_send, cot_recv, slots)
    cot_gather.start()
    half = FF_SHARD // 2
    lo, hi = pl.ds(0, half), pl.ds(half, half)
    loads = [
        pltpu.make_async_copy(w_expand, we.at[0], local.at[0]),
        pltpu.make_async_copy(we_two, we.at[pl.ds(1, 2)], local.at[1]),
        pltpu.make_async_copy(w_reduce, wr.at[0], local.at[2]),
        pltpu.make_async_copy(cot_all, cot_rows.at[:, :, pl.ds(0, D // 2)], local.at[3]),
        pltpu.make_async_copy(cot.at[:, right], cot_rows.at[0, :, right], local.at[4]),
    ]
    for c in loads:
        c.start()
    sib = [
        rcopy(we_two.at[1], we.at[3], w_send.at[0], w_recv.at[0], (SIB,)),
        rcopy(w_reduce, wr.at[1], w_send.at[1], w_recv.at[1], (SIB,)),
        rcopy(wr.at[2], wr.at[3], w_send.at[2], w_recv.at[2], (SIB,)),
    ]
    across = [
        rcopy(w_reduce.at[lo], wr.at[2, lo], w_send.at[3], w_recv.at[3], (XN,)),
        rcopy(w_reduce.at[hi], wr.at[2, hi], w_send.at[4], w_recv.at[4], (XN, 4)),
    ]
    sib[0].start()
    sib[1].start()
    back = {}
    for s in (2, 1, 3, 0):
        for r in range(4):
            place = pl.multiple_of(flip(t, A_MASKS[r] + 2 * s) * ROWS, ROWS)
            src, dst = ctx.at[pl.ds(place, ROWS)], ctx_rows.at[s, r]
            if r:
                back[s, r] = rcopy(src, dst, c_send.at[s, r], c_recv.at[s, r], (A_MASKS[r],))
            else:
                back[s, r] = pltpu.make_async_copy(src, dst, c_send.at[s, r])
    x_low = lax.div(t, 8)

    def start_for(x):
        for own_x, members in ((x, (0, 1)), (1 - x, (2, 3))):

            @pl.when(x_low == own_x)
            def _(members=members):
                for s in (2, 1, 3, 0):
                    for r in members:
                        back[s, r].start()

    attend_kernel(q, k, v, lengths, ctx, {4: lambda: start_for(0)})
    start_for(1)
    cot_gather.forward()
    for c in across:
        c.start()

    def rows_of(s):
        for r in range(4):
            back[s, r].wait_recv() if r else back[s, r].wait()
        return jnp.concatenate([ctx_rows[s, r] for r in range(4)], axis=1)

    for c in late:
        c.wait()
    weight = wo_all[...].reshape(4 * HEAD_DIM, D)

    def ring(index):
        return Ring(
            lambda s, half: parts[{1: 0, 3: 1, 0: 2, 2: 3}[s], half],
            sc_out, sc_pass, sc_got, s_send.at[index], s_recv.at[index], (Y1,), (Y3,), ROWS,
        )

    ring1 = ring(0)
    parts[3] = nn(rows_of(2), weight)
    ring1.opposite()
    three = jnp.concatenate([rows_of(1), rows_of(3), rows_of(0)], axis=0)
    parts[0:3] = nn(three, weight).reshape(3, ROWS, D)
    ring1.neighbours()
    ring1.relay()
    for c in across:
        c.wait_recv()
    sib[2].start()
    for c in loads:
        c.wait()
    ring1.arrive()
    middle = resid[...] + ring1.total(pl.ds(0, ROWS))
    middle_out[...] = middle
    inverse = lax.rsqrt(jnp.mean(middle * middle, axis=-1, keepdims=True) + NORM_EPS)
    mlp_rows[0] = (middle * inverse * gain[...]).astype(BF)
    mlp_gather = Gather(mlp_rows.at[0], mlp_rows, g_send, g_recv, slots)
    mlp_gather.start()
    for s in (1, 3, 2):
        cot_gather.arrived(s)
    shares = [
        rcopy(cot_rows, cot_sib, d_send.at[0], d_recv.at[0], (SIB,)),
        rcopy(mlp_rows, mlp_sib, d_send.at[1], d_recv.at[1], (SIB,)),
    ]
    shares[0].start()
    for c in sib:
        c.wait_recv()

    def block(start, count):
        at, m = pl.ds(start, count), count * ROWS

        @pl.loop(0, 4)
        def _(r):
            expanded = nn(mlp_rows[at].reshape(m, D), we[r])
            grad_active = nt(cot_rows[at].reshape(m, D), wr[r])
            value, slope = gelu_parts(expanded)
            act[r, at] = value.astype(BF).reshape(count, ROWS, FF_SHARD)
            gexp[r, at] = (grad_active * slope).astype(BF).reshape(count, ROWS, FF_SHARD)

    def reduce_rows(start, count):
        at, m = pl.ds(start, count), count * ROWS
        total = nn(act[0, at].reshape(m, FF_SHARD), wr[0])
        for r in range(1, 4):
            total += nn(act[r, at].reshape(m, FF_SHARD), wr[r])
        for i in range(count):
            reduced_out[(0, 1, 3, 2)[start + i]] = total[i * ROWS : (i + 1) * ROWS].astype(BF)

    block(0, 1)
    mlp_gather.forward()
    reduce_rows(0, 1)
    for s in (1, 3):
        mlp_gather.arrived(s)
    block(1, 2)
    mlp_gather.arrived(2)
    shares[1].start()
    block(3, 1)
    for n, r in enumerate((1, 3)):
        shares.append(rcopy(act.at[r], act_sib.at[n], d_send.at[2 + n], d_recv.at[2 + n], (SIB,)))
        shares.append(rcopy(gexp.at[r], gexp_sib.at[n], d_send.at[4 + n], d_recv.at[4 + n], (SIB,)))
    def grad_mlp(start, count):
        at, m = pl.ds(start, count), count * ROWS
        parts[at] = jnp.zeros((count, ROWS, D), F32)

        @pl.loop(0, 4)
        def _(r):
            parts[at] += nt(gexp[r, at].reshape(m, FF_SHARD), we[r]).reshape(count, ROWS, D)

    ring1.finish()
    ring2 = ring(1)
    grad_mlp(3, 1)
    ring2.opposite()
    parts[0:3] = jnp.zeros((3, ROWS, D), F32)

    @pl.loop(0, 4)
    def _(r):
        lhs = jnp.concatenate([gexp[r, 1], gexp[r, 2], gexp[r, 0]], axis=0)
        parts[0:3] += nt(lhs, we[r]).reshape(3, ROWS, D)

    ring2.neighbours()
    for c in shares[2:]:
        c.start()
    ring2.relay()
    reduce_rows(1, 3)
    for c in shares:
        c.wait_recv()
    @pl.loop(0, 8)
    def _(d):
        cols = pl.ds(pl.multiple_of(d * 256, 256), 256)
        own, other = mlp_rows[:, :, cols].reshape(512, 256).T, mlp_sib[:, :, cols].reshape(512, 256).T
        for n, r in enumerate((0, 2)):
            grad_e = nn(own, gexp[r].reshape(512, FF_SHARD)) + nn(other, gexp_sib[n].reshape(512, FF_SHARD))
            for c in range(2):
                stage[n, d, c * 256 : (c + 1) * 256] = grad_e[:, c * 256 : (c + 1) * 256].astype(BF)

    for n, r in enumerate((0, 2)):
        act_turned[n] = jnp.concatenate([act[r].reshape(512, FF_SHARD), act_sib[n].reshape(512, FF_SHARD)], axis=0).T

    @pl.loop(0, 8)
    def _(d):
        cols = pl.ds(pl.multiple_of(d * 256, 256), 256)
        rhs = jnp.concatenate([cot_rows[:, :, cols].reshape(512, 256), cot_sib[:, :, cols].reshape(512, 256)], axis=0)
        for n in range(2):
            stage[n, d, 512:1024] = nn(act_turned[n], rhs).astype(BF)

    keeps = [pltpu.make_async_copy(stage, keep_out, keep_sem)]
    keeps[0].start()
    ring2.arrive()
    got = ring2.total(pl.ds(0, ROWS))
    middle = middle_out[...]
    inverse = lax.rsqrt(jnp.mean(middle * middle, axis=-1, keepdims=True) + NORM_EPS)
    normal = middle * inverse
    grad_gain[...] = jnp.sum(got * normal, axis=0, keepdims=True)
    scaled = got * gain[...]
    grad = cot_rows[0].astype(F32) + inverse * (scaled - normal * jnp.mean(scaled * normal, axis=-1, keepdims=True))
    grad_middle[...] = grad
    grad_low[...] = grad.astype(BF)
    ring2.finish()
    cot_gather.finish()
    mlp_gather.finish()
    for c in sib + across + shares:
        c.wait_send()
    for (s, r), c in back.items():
        if r:
            c.wait_send()
    for c in keeps:
        c.wait()


def mlp(heads, lengths, wo_all, resid, gain_mlp, cot, cot_all, w_expand, we_two, w_reduce):
    dma = pltpu.SemaphoreType.DMA
    vm, hbm, sm = [pl.BlockSpec(memory_space=m) for m in (VMEM, ANY, pltpu.SMEM)]
    return pl.pallas_call(
        mlp_kernel,
        in_specs=[vm, sm, vm] + [hbm] * 7,
        out_specs=[vm, vm, vm, hbm, vm, vm, vm],
        out_shape=[
            jax.ShapeDtypeStruct((4, 4, ROWS, HEAD_DIM), BF),
            jax.ShapeDtypeStruct((ROWS, D), F32),
            jax.ShapeDtypeStruct((4, ROWS, D), BF),
            jax.ShapeDtypeStruct((2, 8, 1024, 256), BF),
            jax.ShapeDtypeStruct((1, D), F32),
            jax.ShapeDtypeStruct((ROWS, D), F32),
            jax.ShapeDtypeStruct((ROWS, D), BF),
        ],
        scratch_shapes=[
            VMEM((2048, HEAD_DIM), BF),
            VMEM((4, D, FF_SHARD), BF),
            VMEM((4, FF_SHARD, D), BF),
            VMEM((4, ROWS, D), BF),
            VMEM((4, ROWS, D), BF),
            VMEM((4, 4, ROWS, FF_SHARD), BF),
            VMEM((4, 4, ROWS, FF_SHARD), BF),
            VMEM((4, ROWS, D), F32),
            VMEM((2, 8, 1024, 256), BF),
            VMEM((3, ROWS, D), BF),
            VMEM((ROWS, D), BF),
            VMEM((2, ROWS, D), BF),
            VMEM((4, ROWS, D), BF),
            VMEM((4, ROWS, D), BF),
            VMEM((2, 4, ROWS, FF_SHARD), BF),
            VMEM((2, 4, ROWS, FF_SHARD), BF),
            VMEM((2, FF_SHARD, 1024), BF),
            dma((6,)), dma((6,)), dma((2, 6)), dma((2, 6)), dma((5,)), dma((5,)), dma((4, 4)), dma((4, 4)),
            dma((6,)), dma((6,)), dma((5,)), dma(()), dma((6,)), dma((6,)),
            VMEM((4, HEAD_DIM, D), BF),
            VMEM((ROWS, D), F32),
            dma((2,)),
        ],
        compiler_params=pltpu.CompilerParams(collective_id=2, has_side_effects=True, vmem_limit_bytes=61 * MIB),
        cost_estimate=pl.CostEstimate(flops=30 * 10**9, bytes_accessed=50 * MIB, transcendentals=0),
        name="mlp",
    )(heads, lengths, gain_mlp[None], wo_all, resid, cot, cot_all, w_expand, we_two, w_reduce)


class Ring:
    def __init__(self, part, out, passed, got, send, recv, near, far, size):
        half = size // 2
        lo, hi = pl.ds(0, half), pl.ds(half, half)

        def c(i, src, dst, target):
            return rcopy(src, dst, send.at[i], recv.at[i], target)

        self.part, self.out, self.passed, self.got, self.lo, self.hi = part, out, passed, got, lo, hi
        self.copies = [
            c(0, out.at[0, lo], passed.at[lo], near),
            c(1, out.at[0, hi], passed.at[hi], far),
            c(2, out.at[1, lo], got.at[0, lo], near),
            c(3, out.at[2, hi], got.at[1, hi], far),
            c(4, out.at[2, lo], got.at[1, lo], far),
            c(5, out.at[1, hi], got.at[0, hi], near),
        ]

    def opposite(self):
        self.send(0, self.lo, self.part(2, self.lo), 0)
        self.send(0, self.hi, self.part(2, self.hi), 1)

    def neighbours(self):
        self.send(1, self.lo, self.part(1, self.lo), 2)
        self.send(2, self.hi, self.part(3, self.hi), 3)

    def begin(self):
        self.opposite()
        self.neighbours()

    def send(self, slot, half, value, i):
        self.out[slot, half] = value.astype(BF)
        self.copies[i].start()

    def relay(self):
        for i, slot, s, half in ((0, 2, 3, self.lo), (1, 1, 1, self.hi)):
            self.copies[i].wait_recv()
            self.out[slot, half] = (self.part(s, half) + self.passed[half].astype(F32)).astype(BF)
            self.copies[4 + i].start()

    def arrive(self):
        for i in (2, 3, 4, 5):
            self.copies[i].wait_recv()

    def total(self, index):
        return self.part(0, index) + self.got[0, index].astype(F32) + self.got[1, index].astype(F32)

    def finish(self):
        for c in self.copies:
            c.wait_send()


X_RING = ((XN,), (XN, 4))
Z_RING = ((0, 1), (0, 3))


class GridSum:
    @staticmethod
    def scratch(rows, pair=True):
        half, dma = rows // 2, pltpu.SemaphoreType.DMA
        return [
            VMEM((2, 8, rows, 256), BF),
            VMEM((2, 8, rows, 256) if pair else (16, 128), BF),
            VMEM((2, 3, 4, half, 256), BF),
            VMEM((2, 4, half, 256), BF),
            VMEM((2, 2, 4, half, 256), BF),
            VMEM((2, 4, half, 256), F32),
            VMEM((2, 3, half, 256), BF),
            VMEM((2, half, 256), BF),
            VMEM((2, 2, half, 256), BF),
            dma((4, 6)),
            dma((4, 6)),
            dma((4,)),
        ]

    def __init__(self, pieces, scratch):
        (self.a, self.b, out1, pass1, got1, self.mid, out2, pass2, got2, send, recv, load) = scratch
        rows = self.a.shape[2]
        self.half = half = rows // 2
        self.loads, start = [], 0
        for i, (kept, given) in enumerate(pieces):
            at = pl.ds(start, kept.shape[2])
            start += kept.shape[2]
            self.loads.append(pltpu.make_async_copy(kept, self.a.at[:, :, at], load.at[2 * i]))
            if given is not None:
                self.loads.append(pltpu.make_async_copy(given, self.b.at[:, :, at], load.at[2 * i + 1]))
        dp = lax.axis_index("dp")
        place = {(sx, sz): flip(dp, (4 if sx in (2, 3) else 0) + sz) for sx in range(4) for sz in range(4)}

        def block(sx, sz, path):
            shard = 0 if sx in (0, 2) else 1
            at = slice(path * half, (path + 1) * half)
            d = place[sx, sz]
            own = self.a[shard, d, at].astype(F32)
            return own if given is None else own + self.b[shard, d, at].astype(F32)

        def span(ds):
            return range(ds.start, ds.start + ds.size)

        def over_x(s, half_):
            return jnp.stack([block(s, z, 0) for z in span(half_)])

        def over_z(s, half_):
            return jnp.stack([block(x, s, 1) for x in span(half_)])

        rings = (X_RING, Z_RING)
        self.first, self.second = [], []
        for path, part in enumerate((over_x, over_z)):
            near, far = rings[path]
            self.first.append(
                Ring(part, out1.at[path], pass1.at[path], got1.at[path], send.at[path], recv.at[path], near, far, 4)
            )
            near, far = rings[1 - path]
            mid = self.mid.at[path]

            def later(s, half_, mid=mid):
                return mid[s, half_]

            self.second.append(
                Ring(
                    later, out2.at[path], pass2.at[path], got2.at[path], send.at[2 + path], recv.at[2 + path], near, far, half
                )
            )

    def load(self):
        for c in self.loads:
            c.start()

    def begin(self):
        for c in self.loads:
            c.wait()
        for ring in self.first:
            ring.begin()

    def relay(self):
        for ring in self.first:
            ring.relay()

    def turn(self):
        for path in range(2):
            ring = self.first[path]
            ring.arrive()
            for s in (2, 1, 3, 0):
                self.mid[path, s] = ring.total(pl.ds(s, 1))[0]
            self.second[path].begin()

    def relay2(self):
        for ring in self.second:
            ring.relay()

    def result(self):
        parts = []
        for ring in self.second:
            ring.arrive()
            parts.append(ring.total(pl.ds(0, self.half)))
        return jnp.concatenate(parts, axis=0)

    def finish(self):
        for ring in self.first + self.second:
            ring.finish()


def back_kernel(
    lengths, grad_low, wo_all, heads_in, ctx_in, reduced_in, middle_in, keep_in,
    output, grads, summed, keep_out, sib_out,
    rows, proj, gc, dk_sum, dv_sum, stage, sc_out, sc_pass, sc_got,
    g_send, g_recv, s_send, s_recv, c_send, c_recv, d_send, d_recv, heads, ctx_rows, reduced, middle, late_sem,
    *grid_scratch,
):
    late = [
        pltpu.make_async_copy(src, dst, late_sem.at[i])
        for i, (src, dst) in enumerate(
            ((heads_in, heads), (ctx_in, ctx_rows), (reduced_in, reduced), (middle_in, middle))
        )
    ]
    for c in late:
        c.start()
    enter([(Y1,), (Y3,), (SIB,), (DIAG,), *X_RING, *Z_RING])
    t = lax.axis_index("tensor")
    gather = Gather(grad_low, rows, g_send, g_recv)
    gather.start()
    part = pl.ds(0, 512)
    grid = GridSum([(keep_in.at[:, :, part], None)], grid_scratch)
    grid.load()
    q, k, v = heads.at[0], heads.at[1], heads.at[2]
    ring = Ring(
        lambda s, half: reduced[s, half].astype(F32), sc_out, sc_pass, sc_got, s_send, s_recv, (Y1,), (Y3,), ROWS
    )
    rows[0] = grad_low[...]
    weight = wo_all[...].reshape(4 * HEAD_DIM, D)
    moves = []

    def project(s):
        y = nt(rows[s], weight).astype(BF)
        place = pl.multiple_of(flip(t, 2 * s) * ROWS, ROWS)
        for r in range(4):
            proj[s, r] = y[:, r * HEAD_DIM : (r + 1) * HEAD_DIM]
            src, dst = proj.at[s, r], gc.at[pl.ds(place, ROWS)]
            if r:
                c = rcopy(src, dst, c_send.at[s, r], c_recv.at[s, r], (A_MASKS[r],))
            else:
                c = pltpu.make_async_copy(src, dst, c_send.at[s, r])
            c.start()
            moves.append((r, c))

    project(0)
    gather.forward()
    for c in late:
        c.wait()
    ring.begin()
    grid.begin()
    for s in (1, 3, 2):
        gather.arrived(s)
        project(s)
    ring.relay()
    grid.relay()
    all_rows = rows[...].reshape(4 * ROWS, D)
    sends = []
    for n, r in enumerate((1, 3, 0, 2)):
        lhs = jnp.concatenate([ctx_rows[s, r] for s in range(4)], axis=0)
        grad_o = tn(lhs, all_rows).astype(BF)
        for d in range(8):
            stage[n, d] = grad_o[:, d * 256 : (d + 1) * 256]
        if n < 2:
            c = rcopy(stage.at[n], sib_out.at[n], d_send.at[n], d_recv.at[n], (SIB,))
        else:
            c = pltpu.make_async_copy(stage.at[n], keep_out.at[n - 2], d_send.at[n])
        c.start()
        sends.append(c)
    for r, c in moves:
        c.wait_recv() if r else c.wait()
    hooks = {4: grid.turn, 7: grid.relay2}
    attend_back_kernel(q, k, v, gc, lengths, grads.at[0], grads.at[1], grads.at[2], dk_sum, dv_sum, hooks)
    summed[...] = grid.result()
    grid.finish()
    ring.arrive()
    output[...] = (middle[...] + ring.total(pl.ds(0, ROWS))).astype(BF)
    gather.finish()
    ring.finish()
    for r, c in moves:
        if r:
            c.wait_send()
    for n, c in enumerate(sends):
        c.wait()


def back(heads, lengths, grad_low, wo_all, ctx_rows, reduced, middle, keep):
    dma = pltpu.SemaphoreType.DMA
    vm, hbm, sm = [pl.BlockSpec(memory_space=m) for m in (VMEM, ANY, pltpu.SMEM)]
    return pl.pallas_call(
        back_kernel,
        in_specs=[sm, vm, vm] + [hbm] * 5,
        out_specs=[vm, vm, vm, hbm, hbm],
        out_shape=[
            jax.ShapeDtypeStruct((ROWS, D), BF),
            jax.ShapeDtypeStruct((3, 2048, HEAD_DIM), BF),
            jax.ShapeDtypeStruct((512, 256), F32),
            jax.ShapeDtypeStruct((2, 8, ROWS, 256), BF),
            jax.ShapeDtypeStruct((2, 8, ROWS, 256), BF),
        ],
        scratch_shapes=[
            VMEM((4, ROWS, D), BF),
            VMEM((4, 4, ROWS, HEAD_DIM), BF),
            VMEM((2048, HEAD_DIM), BF),
            VMEM((2048, HEAD_DIM), F32),
            VMEM((2048, HEAD_DIM), F32),
            VMEM((4, 8, ROWS, 256), BF),
            VMEM((3, ROWS, D), BF),
            VMEM((ROWS, D), BF),
            VMEM((2, ROWS, D), BF),
            dma((6,)), dma((6,)), dma((6,)), dma((6,)), dma((4, 4)), dma((4, 4)), dma((4,)), dma((4,)),
            VMEM((3, 2048, HEAD_DIM), BF),
            VMEM((4, 4, ROWS, HEAD_DIM), BF),
            VMEM((4, ROWS, D), BF),
            VMEM((ROWS, D), F32),
            dma((4,)),
            *GridSum.scratch(512, False),
        ],
        compiler_params=pltpu.CompilerParams(collective_id=3, has_side_effects=True, vmem_limit_bytes=61 * MIB),
        cost_estimate=pl.CostEstimate(flops=8 * 10**9, bytes_accessed=20 * MIB, transcendentals=0),
        name="back",
    )(lengths, grad_low, wo_all, heads, ctx_rows, reduced, middle, keep)


def streams_kernel(
    grads, rows_in, w_in, keep_in, hist_in, middle_in, normal_in, inv, gain_q, gain_k, gain_v,
    ds, mixed, newest, sums, summed, keep_out, sib_out,
    hist, hist_sem, rows, weights, g, turned, parts, stage, sc_out, sc_pass, sc_got,
    s_send, s_recv, c_send, c_recv, d_send, d_recv, local, grad_middle, n_in, late_sem, *grid_scratch,
):
    late = [
        pltpu.make_async_copy(middle_in, grad_middle, late_sem.at[0]),
        pltpu.make_async_copy(normal_in, n_in, late_sem.at[1]),
    ]
    for c in late:
        c.start()
    enter([(Y1,), (Y3,), (SIB,), (DIAG,), *X_RING, *Z_RING])
    t = lax.axis_index("tensor")
    part = pl.ds(512, 512)
    grid = GridSum([(keep_in.at[:, :, part], None)], grid_scratch)
    moves = {}
    for a in range(3):
        for s in (2, 1, 3, 0):
            for r in range(4):
                place = pl.multiple_of(flip(t, A_MASKS[r] + 2 * s) * ROWS, ROWS)
                src, dst = grads.at[a, pl.ds(place, ROWS)], g.at[a, s, r]
                if r:
                    c = rcopy(src, dst, c_send.at[a, s, r], c_recv.at[a, s, r], (A_MASKS[r],))
                else:
                    c = pltpu.make_async_copy(src, dst, c_send.at[a, s, r])
                c.start()
                moves[a, s, r] = c
    gains = (gain_q, gain_k, gain_v)
    tiles = ROWS // STEP
    lane = lax.broadcasted_iota(jnp.int32, (STEP, 256), 1)
    own = lax.rem(lane, STEP) == lax.broadcasted_iota(jnp.int32, (STEP, 256), 0)
    column = lax.broadcasted_iota(jnp.int32, (STEP, 128), 1)
    newest[...] = jnp.zeros(newest.shape, F32)

    def tile_load(tile):
        at = pl.ds(pl.multiple_of(tile * STEP, STEP), STEP)
        slot = lax.rem(tile, 2)
        return pltpu.make_async_copy(hist_in.at[:, at], hist.at[slot], hist_sem.at[slot])

    def rows_of_mixing(streams):
        tile_load(jnp.int32(0)).start()

        def step(tile, totals):
            at = pl.ds(pl.multiple_of(tile * STEP, STEP), STEP)

            @pl.when(tile < tiles - 1)
            def _():
                tile_load(tile + 1).start()

            totals, values = list(totals), []
            for i, k in enumerate(streams):
                if k == 3:
                    values.append(grad_middle[at])
                    continue
                grad, normal = rings[k].total(at), n_in[k, at].astype(F32)
                product = grad * normal
                totals[i] = totals[i] + product[:8] + product[8:]
                scaled = grad * gains[k][...]
                mean = jnp.sum(scaled * normal, axis=-1, keepdims=True) * (1.0 / D)
                value = (scaled - normal * mean) * inv[k, at, 0:1]
                ds[k, at] = value.astype(BF)
                values.append(value)
            split = [halves(value) for value in values]
            left = jnp.concatenate([h for h, _ in split] + [m for _, m in split], axis=0)
            tile_load(tile).wait()
            slot = lax.rem(tile, 2)
            product = nt(left, hist[slot, 0 : HISTORY - 1].reshape(256, D))
            last = hist[slot, HISTORY - 1].astype(F32)
            count = len(streams)
            for i, k in enumerate(streams):
                both = product[i * STEP : (i + 1) * STEP] + product[(count + i) * STEP : (count + i + 1) * STEP]
                mixed[k, at] = jnp.where(own, both, 0.0)
                newest[at] = jnp.where(column == k, jnp.sum(values[i] * last, axis=-1, keepdims=True), newest[at])
            return tuple(totals)

        totals = lax.fori_loop(0, tiles, step, (jnp.zeros((8, D), F32),) * len(streams))
        for total, k in zip(totals, streams):
            if k < 3:
                sums[k : k + 1] = jnp.sum(total, axis=0, keepdims=True)

    loads = []
    for a in range(3):
        c = pltpu.make_async_copy(w_in.at[a], weights.at[a], local.at[a])
        c.start()
        loads.append(c)
    for a in range(3):
        loads.append(pltpu.make_async_copy(rows_in.at[a], rows, local.at[3 + a]))
    loads[3].start()
    grid.load()
    rings = [
        Ring(
            lambda s, half, a=a: parts[a, pl.ds({0: 0, 1: 64, 3: 192}[s] + half.start, half.size)],
            sc_out.at[a], sc_pass.at[a], sc_got.at[a], s_send.at[a], s_recv.at[a], (Y1,), (Y3,), ROWS,
        )
        for a in range(3)
    ]

    def left_of(a, s):
        for r in range(4):
            c = moves[a, s, r]
            c.wait_recv() if r else c.wait()
        return jnp.concatenate([g[a, s, r] for r in range(4)], axis=1)

    def opposite(a):
        loads[a].wait()
        weight = jnp.concatenate([weights[a, r] for r in range(4)], axis=1)
        value, ring = nt(left_of(a, 2), weight), rings[a]
        ring.send(0, ring.lo, value[:64], 0)
        ring.send(0, ring.hi, value[64:], 1)

    def neighbours(a):
        weight = jnp.concatenate([weights[a, r] for r in range(4)], axis=1)
        ring = rings[a]
        value = nt(jnp.concatenate([left_of(a, 1), left_of(a, 3), left_of(a, 0)], axis=0), weight)
        ring.send(1, ring.lo, value[:64], 2)
        ring.send(2, ring.hi, value[192:256], 3)
        parts[a, 128:192] = value[64:128]
        parts[a, 192:256] = value[128:192]
        parts[a, 0:128] = value[256:384]

    def weight_gradient(a):
        loads[3 + a].wait()
        turned[...] = rows[...].reshape(512, D).T
        if a < 2:
            loads[4 + a].start()
        grad_w = nn(
            turned[...], jnp.concatenate([g[a, :, r].reshape(512, HEAD_DIM) for r in range(4)], axis=1)
        ).astype(BF)
        for n, r in enumerate((1, 3, 0, 2)):
            for d in range(8):
                block = grad_w[d * 256 : (d + 1) * 256, r * HEAD_DIM : (r + 1) * HEAD_DIM]
                if a < 2:
                    stage[n, d, 0:256, a * 128 : (a + 1) * 128] = block
                else:
                    stage[n, d, 256:384, 0:128] = block[:128]
                    stage[n, d, 256:384, 128:256] = block[128:]

    opposite(0)
    neighbours(0)
    opposite(1)
    grid.begin()
    rings[0].relay()
    neighbours(1)
    opposite(2)
    weight_gradient(0)
    weight_gradient(1)
    rings[1].relay()
    neighbours(2)
    grid.relay()
    weight_gradient(2)
    for c in late:
        c.wait()
    rings[0].arrive()
    rows_of_mixing((0, 3))
    grid.turn()
    rings[2].relay()
    sends = []
    for n in range(4):
        if n < 2:
            c = rcopy(stage.at[n], sib_out.at[n], d_send.at[n], d_recv.at[n], (SIB,))
        else:
            c = pltpu.make_async_copy(stage.at[n], keep_out.at[n - 2], d_send.at[n])
        c.start()
        sends.append(c)
    grid.relay2()
    rings[1].arrive()
    rows_of_mixing((1,))
    summed[...] = grid.result()
    grid.finish()
    rings[2].arrive()
    rows_of_mixing((2,))
    for ring in rings:
        ring.finish()
    for (a, s, r), c in moves.items():
        if r:
            c.wait_send()
    for c in sends:
        c.wait()


def streams_back(grads, rows, w_all, keep, history, grad_middle, n, inv, gains):
    dma = pltpu.SemaphoreType.DMA
    vm, hbm = pl.BlockSpec(memory_space=VMEM), pl.BlockSpec(memory_space=ANY)
    return pl.pallas_call(
        streams_kernel,
        in_specs=[vm] + [hbm] * 6 + [vm] * 4,
        out_specs=[vm] * 5 + [hbm] * 2,
        out_shape=[
            jax.ShapeDtypeStruct((3, ROWS, D), BF),
            jax.ShapeDtypeStruct((4, ROWS, 256), F32),
            jax.ShapeDtypeStruct((ROWS, 128), F32),
            jax.ShapeDtypeStruct((3, D), F32),
            jax.ShapeDtypeStruct((512, 256), F32),
            jax.ShapeDtypeStruct((2, 8, 384, 256), BF),
            jax.ShapeDtypeStruct((2, 8, 384, 256), BF),
        ],
        scratch_shapes=[
            VMEM((2, HISTORY, STEP, D), BF),
            dma((2,)),
            VMEM((4, ROWS, D), BF),
            VMEM((3, 4, D, HEAD_DIM), BF),
            VMEM((3, 4, 4, ROWS, HEAD_DIM), BF),
            VMEM((D, 512), BF),
            VMEM((3, 256, D), F32),
            VMEM((4, 8, 384, 256), BF),
            VMEM((3, 3, ROWS, D), BF),
            VMEM((3, ROWS, D), BF),
            VMEM((3, 2, ROWS, D), BF),
            dma((3, 6)), dma((3, 6)), dma((3, 4, 4)), dma((3, 4, 4)), dma((4,)), dma((4,)), dma((6,)),
            VMEM((ROWS, D), F32),
            VMEM((3, ROWS, D), BF),
            dma((2,)),
            *GridSum.scratch(512, False),
        ],
        compiler_params=pltpu.CompilerParams(collective_id=4, has_side_effects=True, vmem_limit_bytes=61 * MIB),
        cost_estimate=pl.CostEstimate(flops=8 * 10**9, bytes_accessed=20 * MIB, transcendentals=0),
        name="streams_back",
    )(grads, rows, w_all, keep, history, grad_middle, n, inv, *[x[None] for x in gains])


SMALL_ROWS, SMALL_COLS = 80, D + 128
NEAR = [(m, 0) for m in range(1, 8)]
FAR = [(XN if m // 4 in (1, 3) else 0, (4 if m // 4 in (2, 3) else 0) + m % 4) for m in range(1, 16)]
TILES = 11


def finish_kernel(
    hist_in, mixed, newest, sums, pre, mix_gain, mix_first, mix_second, gain_mlp,
    keep_q, sib_q, keep_o, sib_o,
    extra, summed, small_out,
    hist, pack, acc, acc1, near_out, near_got, far_out, far_got,
    res, hist_sem, r_send, r_recv, a_send, a_recv, *grid_scratch,
):
    load = pltpu.make_async_copy(hist_in.at[HISTORY - 1], hist, hist_sem)
    load.start()
    enter(NEAR + FAR)
    grid = GridSum([(keep_q, sib_q), (keep_o, sib_o)], grid_scratch)
    grid.load()
    t, dp = lax.axis_index("tensor"), lax.axis_index("dp")
    near = lax.rem(t, 8)
    far = 4 * (2 * lax.div(dp, 4) + lax.div(t, 8)) + lax.rem(dp, 4)
    grid.begin()
    load.wait()

    place = lax.broadcasted_iota(jnp.int32, (256, MIX), 1)
    entry = lax.div(lax.broadcasted_iota(jnp.int32, (256, MIX), 0), STEP)
    column = lax.broadcasted_iota(jnp.int32, (ROWS, MIX), 1)
    grad_mixing = jnp.zeros((ROWS, MIX), F32)
    for k in range(STREAMS):
        gathered = exact(mixed[k], (place == entry + k * HISTORY).astype(F32), ((1,), (0,)))
        grad_mixing = grad_mixing + gathered
        grad_mixing = jnp.where(column == k * HISTORY + HISTORY - 1, newest[:, k : k + 1], grad_mixing)
    hidden, slope = gelu_parts(pre[...])
    last = hist[...].astype(F32)
    inverse = lax.rsqrt(jnp.mean(last * last, axis=-1, keepdims=True) + NORM_EPS)
    normal = last * inverse
    grad_pre = exact(grad_mixing, mix_second[...], ((1,), (1,))) * slope
    pack[...] = jnp.zeros(pack.shape, F32)
    pack[0:MIX, 0:D] = exact(grad_pre, normal * mix_gain[...], ((0,), (0,)))
    pack[0:MIX, D : D + MIX] = exact(hidden, grad_mixing, ((0,), (0,)))
    grad_latest = exact(grad_pre, mix_first[...], ((1,), (0,)))
    pack[68:69, 0:D] = jnp.sum(grad_latest * normal, axis=0, keepdims=True)
    pack[69:72, 0:D] = sums[...]
    pack[72:73, 0:D] = gain_mlp[...]
    pack[68:69, D : D + MIX] = jnp.sum(grad_mixing, axis=0, keepdims=True)
    scaled = grad_latest * mix_gain[...]
    extra[...] = inverse * (scaled - normal * jnp.mean(scaled * normal, axis=-1, keepdims=True))
    acc[7, TILES - 3 : TILES] = jnp.zeros((3, 16, 128), F32)
    acc1[TILES:16] = jnp.zeros((16 - TILES, 16, 128), F32)
    columns = SMALL_COLS // 128
    for i in range(SMALL_ROWS // 16):
        for j in range(columns):
            b = i * columns + j
            acc[b // TILES, b % TILES] = pack[i * 16 : (i + 1) * 16, j * 128 : (j + 1) * 128]

    def exchange(targets, sources, places, level):
        copies = []
        for i, target in enumerate(targets):
            c = rcopy(sources(i), places(i), level[0].at[i], level[1].at[i], target)
            c.start()
            copies.append(c)
        return copies

    near_out[...] = acc[...].astype(BF)
    copies = exchange(NEAR, lambda i: near_out.at[flip(near, i + 1)], lambda i: near_got.at[i], (r_send.at[0], r_recv.at[0]))
    grid.relay()
    for c in copies:
        c.wait()
    total = acc[near]
    for i in range(7):
        total = total + near_got[i].astype(F32)
    acc1[0:TILES] = total
    far_out[...] = acc1[...].astype(BF)
    copies = exchange(FAR, lambda i: far_out.at[flip(far, i + 1)], lambda i: far_got.at[i], (r_send.at[1], r_recv.at[1]))
    for c in copies:
        c.wait()
    total = acc1[far]
    for i in range(15):
        total = total + far_got[i].astype(F32)
    res[near, far] = total.astype(BF)
    mine = res.at[near, far]
    copies = exchange(FAR, lambda i: mine, lambda i: mine, (a_send.at[1], a_recv.at[1]))
    grid.turn()
    for c in copies:
        c.wait()
    mine_all = res.at[near, pl.ds(0, TILES)]
    copies = exchange(NEAR, lambda i: mine_all, lambda i: mine_all, (a_send.at[0], a_recv.at[0]))
    grid.relay2()
    for c in copies:
        c.wait()
    for i in range(SMALL_ROWS // 16):
        for j in range(columns):
            b = i * columns + j
            small_out[i * 16 : (i + 1) * 16, j * 128 : (j + 1) * 128] = res[b // TILES, b % TILES].astype(F32)
    summed[...] = grid.result()
    grid.finish()


def finish(history, mixed, newest, sums, pre, mix_gain, mix_first, mix_second, gain_mlp, *packs):
    dma = pltpu.SemaphoreType.DMA
    vm, hbm = pl.BlockSpec(memory_space=VMEM), pl.BlockSpec(memory_space=ANY)
    tile = (16, 128)
    return pl.pallas_call(
        finish_kernel,
        in_specs=[hbm] + [vm] * 8 + [hbm] * 4,
        out_specs=[vm] * 3,
        out_shape=[
            jax.ShapeDtypeStruct((ROWS, D), F32),
            jax.ShapeDtypeStruct((512, 256), F32),
            jax.ShapeDtypeStruct((SMALL_ROWS, SMALL_COLS), F32),
        ],
        scratch_shapes=[
            VMEM((ROWS, D), BF),
            VMEM((SMALL_ROWS, SMALL_COLS), F32),
            VMEM((8, TILES, *tile), F32),
            VMEM((16, *tile), F32),
            VMEM((8, TILES, *tile), BF),
            VMEM((7, TILES, *tile), BF),
            VMEM((16, *tile), BF),
            VMEM((15, *tile), BF),
            VMEM((8, 16, *tile), BF),
            dma(()), dma((2, 15)), dma((2, 15)), dma((2, 15)), dma((2, 15)),
            *GridSum.scratch(512),
        ],
        compiler_params=pltpu.CompilerParams(collective_id=5, has_side_effects=True, vmem_limit_bytes=61 * MIB),
        cost_estimate=pl.CostEstimate(flops=10**9, bytes_accessed=30 * MIB, transcendentals=0),
        name="finish",
    )(history, mixed, newest, sums, pre, mix_gain[None], mix_first.T, mix_second, gain_mlp, *packs)


def last_kernel(
    ds, grad_low, extra, mix, small, sum_a, sum_e, sum_r, low,
    grad_hist, g_first, g_second, g_bias, g_mix, g_query, g_key, g_value, g_mlp, gw_q, gw_k, gw_v, gw_o, gw_e, gw_r, output,
):
    rows = ds.shape[1]

    @pl.when(pl.program_id(0) == 0)
    def _():
        g_first[...] = small[0:MIX, :D]
        g_second[...] = small[0:MIX, D : D + MIX]
        g_bias[...] = small[68:69, D : D + MIX]
        for i, ref in enumerate((g_mix, g_query, g_key, g_value, g_mlp)):
            ref[...] = small[68 + i : 69 + i, :D]
        gw_q[...] = sum_a[:256, :128]
        gw_k[...] = sum_a[:256, 128:]
        gw_v[:128] = sum_a[256:384, :128]
        gw_v[128:] = sum_a[256:384, 128:]
        gw_o[...] = sum_a[384:]
        gw_e[:, :256] = sum_e[:256]
        gw_e[:, 256:] = sum_e[256:]
        gw_r[...] = sum_r[...]
        output[...] = low[...]

    here = mix[...]
    lane = lax.broadcasted_iota(jnp.int32, (rows, 128), 1)
    own = lax.rem(lane, rows) == lax.broadcasted_iota(jnp.int32, (rows, 128), 0)
    stream = lax.rem(lax.div(lane, rows), STREAMS)
    left = []
    for j in range(HISTORY):
        piece = jnp.zeros((rows, 128), F32)
        for k in range(STREAMS):
            i = k * HISTORY + j
            piece = jnp.where(stream == k, here[:, i : i + 1], piece)
        high, low = halves(jnp.where(own, piece, 0.0))
        left.append(jnp.where(lane < 64, high.astype(F32), low.astype(F32)).astype(BF))
    left = jnp.concatenate(left, axis=0)
    for c in range(D // 512):
        cols = slice(c * 512, (c + 1) * 512)
        right = jnp.concatenate([ds[k, :, cols] if k < 3 else grad_low[:, cols] for k in range(STREAMS)], axis=0)
        product = nn(left, jnp.concatenate([right, right], axis=0))
        grad_hist[0 : HISTORY - 1, :, cols] = product[:256].astype(BF).reshape(HISTORY - 1, rows, 512)
        grad_hist[HISTORY - 1, :, cols] = (product[256:] + extra[:, cols]).astype(BF)


def last(ds, grad_low, extra, mix, small, sum_a, sum_e, sum_r, output):
    rows = 16

    def whole(*shape):
        return pl.BlockSpec(shape, lambda i: (0,) * len(shape))

    shapes = [(MIX, D), (MIX, MIX), (1, MIX)] + [(1, D)] * 5
    shapes += [(256, 128)] * 3 + [(128, 256), (256, 512), (512, 256)]
    return pl.pallas_call(
        last_kernel,
        grid=(ROWS // rows,),
        in_specs=[
            pl.BlockSpec((3, rows, D), lambda i: (0, i, 0)),
            pl.BlockSpec((rows, D), lambda i: (i, 0)),
            pl.BlockSpec((rows, D), lambda i: (i, 0)),
            pl.BlockSpec((rows, MIX), lambda i: (i, 0)),
            whole(SMALL_ROWS, SMALL_COLS),
            whole(512, 256),
            whole(512, 256),
            whole(512, 256),
            whole(ROWS, D),
        ],
        out_specs=[pl.BlockSpec((HISTORY, rows, D), lambda i: (0, i, 0))] + [whole(*x) for x in shapes] + [whole(ROWS, D)],
        out_shape=[jax.ShapeDtypeStruct((HISTORY, ROWS, D), BF)]
        + [jax.ShapeDtypeStruct(x, F32) for x in shapes]
        + [jax.ShapeDtypeStruct((ROWS, D), BF)],
        compiler_params=pltpu.CompilerParams(vmem_limit_bytes=61 * MIB),
        name="last",
    )(ds, grad_low, extra, mix, small, sum_a, sum_e, sum_r, output)


def on_device(
    history, cotangent, lengths, mix_gain, mix_first, mix_second, mix_bias,
    gain_query, gain_key, gain_value, gain_mlp, w_query, w_key, w_value, w_output, w_expand, w_reduce,
):
    gains = (gain_query, gain_key, gain_value)
    heads, rows, w_all, wo_all, we_two, cot_all, n, inv, resid, mix, pre = qkv(
        history, cotangent, mix_gain, mix_first, mix_second, mix_bias, gains, w_query, w_key, w_value, w_output, w_expand
    )
    heads = heads.reshape(3, 2048, HEAD_DIM)
    ctx_rows, middle, reduced, keep_mlp, g_gain_mlp, grad_middle, grad_low = mlp(
        heads, lengths, wo_all, resid, gain_mlp, cotangent, cot_all, w_expand, we_two, w_reduce
    )
    output, grads, sum_e, keep_o, sib_o = back(heads, lengths, grad_low, wo_all, ctx_rows, reduced, middle, keep_mlp)
    ds, mixed, newest, sums, sum_r, keep_q, sib_q = streams_back(
        grads, rows, w_all, keep_mlp, history, grad_middle, n, inv, gains
    )
    extra, sum_a, small = finish(
        history, mixed, newest, sums, pre, mix_gain, mix_first, mix_second, g_gain_mlp, keep_q, sib_q, keep_o, sib_o
    )
    outs = last(ds, grad_low, extra, mix, small, sum_a, sum_e, sum_r, output)
    grad_history, g_first, g_second, g_bias, g_mix, g_query, g_key, g_value, g_mlp = outs[:9]
    return (
        outs[15], grad_history, g_mix[0], g_first.T, g_second, g_bias[0], g_query[0], g_key[0], g_value[0], g_mlp[0],
        *outs[9:15],
    )


def solution(mesh):
    rows, cols, both = P("tensor", None), P(None, "tensor"), ("dp", "tensor")
    return jax.shard_map(
        on_device,
        mesh=mesh,
        in_specs=(P(None, both, None), P(both, None)) + (P(),) * 9 + (cols, cols, cols, rows, cols, rows),
        out_specs=(P(both, None), P(None, both, None)) + (P(),) * 8
        + (P("dp", "tensor"),) * 3 + (P("tensor", "dp"), P("dp", "tensor"), P("tensor", "dp")),
        check_vma=False,
    )
```

profile of v0, /device:TPU:1, one launch (start us, length us, event | category | flops | bytes accessed | tf_op | source)
XLA Modules:
  0.0 353.3 jit_solution(1337304256692922795)
XLA Ops:
  0.6 1.3 copy.34.lengths
  2.0 74.4 %qkv.1 = (bf16[3,16,128,128]{3,2,1,0:T(8,128)(2,1)}, bf16[3,4,128,2048]{3,2,1,0:T(8,128)(2,1)}, bf16[3,4,2048,128]{3,2,1,0:T(8,128)(2,1)}, bf16[4,128,2048]{2,1,...) custom-call(bf16[17,128,2048]{2,1,0:T(8,128)(2,1)} %hist_in.5, ...), custom_call_target="tpu_custom_call" | custom-call | flops 3221225472 | bytes 31457280 | tf_op jit(solution)/shard_map/qkv/pallas_call | solution.py:322
  76.4 91.0 %mlp.1 = (bf16[4,4,128,128]{3,2,1,0:T(8,128)(2,1)}, f32[128,2048]{1,0:T(8,128)}, bf16[4,128,2048]{2,1,0:T(8,128)(2,1)}, bf16[2,8,1024,256]{3,2,1,0:T(8,128)(2,1)...) custom-call(bf16[3,2048,128]{2,1,0:T(8,128)(2,1)} %bitcast.26, s32[8,4]{1,0:T(8,128)} %copy.34.lengths, ...), custom_call_target="tpu_custom_call" | custom-call | flops 30000001024 | bytes 52428800 | tf_op jit(solution)/shard_map/mlp/pallas_call | solution.py:633
  167.4 53.9 %back.1 = (bf16[128,2048]{1,0:T(8,128)(2,1)}, bf16[3,2048,128]{2,1,0:T(8,128)(2,1)}, f32[512,256]{1,0:T(8,128)}, bf16[2,8,128,256]{3,2,1,0:T(8,128)(2,1)}, bf16[2,8,128,256]{3,2,1,0:T(8,128)(2,1)}) custom-call(s32[8,4]{1,0:T(8,128)} %copy.34.lengths, bf16[128,2048]{1,0:T(8,128)(2,1)} %get-tuple-element.70.grad_low, ...), custom_call_target="tpu_custom_call" | custom-call | flops 8000000000 | bytes 20971520 | tf_op jit(solution)/shard_map/back/pallas_call | solution.py:925
  221.3 76.9 %streams_back.1 = (bf16[3,128,2048]{2,1,0:T(8,128)(2,1)}, f32[4,128,256]{2,1,0:T(8,128)}, f32[128,128]{1,0:T(8,128)}, f32[3,2048]{1,0:T(4,128)}, f32[512,256]{1,...) custom-call(bf16[3,2048,128]{2,1,0:T(8,128)(2,1)} %get-tuple-element.75.grads, ...), custom_call_target="tpu_custom_call" | custom-call | flops 8000000000 | bytes 20971520 | tf_op jit(solution)/shard_map/streams_back/pallas_call | solution.py:1144
  298.3 42.7 %finish.1 = (f32[128,2048]{1,0:T(8,128)}, f32[512,256]{1,0:T(8,128)}, f32[80,2176]{1,0:T(8,128)}) custom-call(bf16[17,128,2048]{2,1,0:T(8,128)(2,1)} %hist_in.5, f32[4,128,256]{2,1,0:T(8,128)} %get-tuple-element.82.mixed, f32[128,128]{1,0:T(8,128)} %get-tuple-element.83.newest, f32[3,2048]{1,0:T(4,128)} %get-tuple-element.84.sums, ...), custom_call_target="tpu_custom_call" | custom-call | flops 1000000000 | bytes 31457280 | tf_op jit(solution)/shard_map/finish/pallas_call | solution.py:1283
  341.0 11.9 %last.1 = (bf16[17,128,2048]{2,1,0:T(8,128)(2,1)}, f32[68,2048]{1,0:T(8,128)}, f32[68,68]{1,0:T(8,128)}, f32[1,68]{1,0:T(1,128)}, f32[1,2048]{1,0:T(1,128)}, /*i...) custom-call(bf16[3,128,2048]{2,1,0:T(8,128)(2,1)} %get-tuple-element, ...), custom_call_target="tpu_custom_call" | custom-call | tf_op jit(solution)/shard_map/last/pallas_call | solution.py:1363
where the time goes:
time: 360 us; the launch traced here: 353 us
  Pallas kernels  351 us (98%)
    pallas_call x1, Pallas kernels, mlp(): pl.pallas_call(mlp_kernel, in_specs=[vm, sm, vm] + [hbm] * 7, out_specs=[...  91 us
    pallas_call x1, Pallas kernels, streams_back(): pl.pallas_call(streams_kernel, in_specs=[vm] + [hbm] * 6 + [vm] * 4, out_...  76.9 us
    pallas_call x1, Pallas kernels, qkv(): pl.pallas_call(qkv_kernel, in_specs=[hbm] * 2 + [vm] * 7 + [hbm] * 5, out...  74.4 us
    pallas_call x1, Pallas kernels, back(): pl.pallas_call(back_kernel, in_specs=[sm, vm, vm] + [hbm] * 5, out_specs=...  53.9 us
    pallas_call x1, Pallas kernels, finish(): pl.pallas_call(finish_kernel, in_specs=[hbm] + [vm] * 8 + [hbm] * 4, out_...  42.7 us
    pallas_call x1, Pallas kernels, last(): pl.pallas_call(last_kernel, grid=(ROWS // rows,), in_specs=[pl.BlockSpec(...  11.9 us

commit v1 on v0

--- a/solution.py
+++ b/solution.py
@@ -552,6 +552,7 @@
     for s in (1, 3):
         mlp_gather.arrived(s)
     block(1, 2)
+    reduce_rows(1, 2)
     mlp_gather.arrived(2)
     shares[1].start()
     block(3, 1)
@@ -581,7 +582,7 @@
     for c in shares[2:]:
         c.start()
     ring2.relay()
-    reduce_rows(1, 3)
+    reduce_rows(3, 1)
     for c in shares:
         c.wait_recv()
     @pl.loop(0, 8)
@@ -1215,6 +1216,7 @@
     inverse = lax.rsqrt(jnp.mean(last * last, axis=-1, keepdims=True) + NORM_EPS)
     normal = last * inverse
     grad_pre = exact(grad_mixing, mix_second[...], ((1,), (1,))) * slope
+    grid.relay()
     pack[...] = jnp.zeros(pack.shape, F32)
     pack[0:MIX, 0:D] = exact(grad_pre, normal * mix_gain[...], ((0,), (0,)))
     pack[0:MIX, D : D + MIX] = exact(hidden, grad_mixing, ((0,), (0,)))
@@ -1243,7 +1245,6 @@
 
     near_out[...] = acc[...].astype(BF)
     copies = exchange(NEAR, lambda i: near_out.at[flip(near, i + 1)], lambda i: near_got.at[i], (r_send.at[0], r_recv.at[0]))
-    grid.relay()
     for c in copies:
         c.wait()
     total = acc[near]

time: 360 us -> 361 us (level)
  no operation moved by 1% of the time
where the time goes in v1:
time: 361 us; the launch traced here: 354 us
  Pallas kernels  352 us (98%)
    pallas_call x1, Pallas kernels, mlp(): pl.pallas_call(mlp_kernel, in_specs=[vm, sm, vm] + [hbm] * 7, out_specs=[...  93.4 us
    pallas_call x1, Pallas kernels, streams_back(): pl.pallas_call(streams_kernel, in_specs=[vm] + [hbm] * 6 + [vm] * 4, out_...  77 us
    pallas_call x1, Pallas kernels, qkv(): pl.pallas_call(qkv_kernel, in_specs=[hbm] * 2 + [vm] * 7 + [hbm] * 5, out...  74.4 us
    pallas_call x1, Pallas kernels, back(): pl.pallas_call(back_kernel, in_specs=[sm, vm, vm] + [hbm] * 5, out_specs=...  52.3 us
    pallas_call x1, Pallas kernels, finish(): pl.pallas_call(finish_kernel, in_specs=[hbm] + [vm] * 8 + [hbm] * 4, out_...  42.6 us
    pallas_call x1, Pallas kernels, last(): pl.pallas_call(last_kernel, grid=(ROWS // rows,), in_specs=[pl.BlockSpec(...  11.9 us

profile of v1, /device:TPU:1, one launch (start us, length us, event | category | flops | bytes accessed | tf_op | source)
XLA Modules:
  0.0 354.0 jit_solution(4460837146515365003)
XLA Ops:
  0.6 1.3 copy.34.lengths
  2.0 74.4 %qkv.1 = (bf16[3,16,128,128]{3,2,1,0:T(8,128)(2,1)}, bf16[3,4,128,2048]{3,2,1,0:T(8,128)(2,1)}, bf16[3,4,2048,128]{3,2,1,0:T(8,128)(2,1)}, bf16[4,128,2048]{2,1,...) custom-call(bf16[17,128,2048]{2,1,0:T(8,128)(2,1)} %hist_in.5, ...), custom_call_target="tpu_custom_call" | custom-call | flops 3221225472 | bytes 31457280 | tf_op jit(solution)/shard_map/qkv/pallas_call | solution.py:322
  76.4 93.4 %mlp.1 = (bf16[4,4,128,128]{3,2,1,0:T(8,128)(2,1)}, f32[128,2048]{1,0:T(8,128)}, bf16[4,128,2048]{2,1,0:T(8,128)(2,1)}, bf16[2,8,1024,256]{3,2,1,0:T(8,128)(2,1)...) custom-call(bf16[3,2048,128]{2,1,0:T(8,128)(2,1)} %bitcast.26, s32[8,4]{1,0:T(8,128)} %copy.34.lengths, ...), custom_call_target="tpu_custom_call" | custom-call | flops 30000001024 | bytes 52428800 | tf_op jit(solution)/shard_map/mlp/pallas_call | solution.py:634
  169.8 52.3 %back.1 = (bf16[128,2048]{1,0:T(8,128)(2,1)}, bf16[3,2048,128]{2,1,0:T(8,128)(2,1)}, f32[512,256]{1,0:T(8,128)}, bf16[2,8,128,256]{3,2,1,0:T(8,128)(2,1)}, bf16[2,8,128,256]{3,2,1,0:T(8,128)(2,1)}) custom-call(s32[8,4]{1,0:T(8,128)} %copy.34.lengths, bf16[128,2048]{1,0:T(8,128)(2,1)} %get-tuple-element.70.grad_low, ...), custom_call_target="tpu_custom_call" | custom-call | flops 8000000000 | bytes 20971520 | tf_op jit(solution)/shard_map/back/pallas_call | solution.py:926
  222.1 77.0 %streams_back.1 = (bf16[3,128,2048]{2,1,0:T(8,128)(2,1)}, f32[4,128,256]{2,1,0:T(8,128)}, f32[128,128]{1,0:T(8,128)}, f32[3,2048]{1,0:T(4,128)}, f32[512,256]{1,...) custom-call(bf16[3,2048,128]{2,1,0:T(8,128)(2,1)} %get-tuple-element.75.grads, ...), custom_call_target="tpu_custom_call" | custom-call | flops 8000000000 | bytes 20971520 | tf_op jit(solution)/shard_map/streams_back/pallas_call | solution.py:1145
  299.1 42.6 %finish.1 = (f32[128,2048]{1,0:T(8,128)}, f32[512,256]{1,0:T(8,128)}, f32[80,2176]{1,0:T(8,128)}) custom-call(bf16[17,128,2048]{2,1,0:T(8,128)(2,1)} %hist_in.5, f32[4,128,256]{2,1,0:T(8,128)} %get-tuple-element.82.mixed, f32[128,128]{1,0:T(8,128)} %get-tuple-element.83.newest, f32[3,2048]{1,0:T(4,128)} %get-tuple-element.84.sums, ...), custom_call_target="tpu_custom_call" | custom-call | flops 1000000000 | bytes 31457280 | tf_op jit(solution)/shard_map/finish/pallas_call | solution.py:1284
  341.7 11.9 %last.1 = (bf16[17,128,2048]{2,1,0:T(8,128)(2,1)}, f32[68,2048]{1,0:T(8,128)}, f32[68,68]{1,0:T(8,128)}, f32[1,68]{1,0:T(1,128)}, f32[1,2048]{1,0:T(1,128)}, /*i...) custom-call(bf16[3,128,2048]{2,1,0:T(8,128)(2,1)} %get-tuple-element, ...), custom_call_target="tpu_custom_call" | custom-call | tf_op jit(solution)/shard_map/last/pallas_call | solution.py:1364
